TPU v7x, 32 devices: a whole 2x2x4 slice. The times are simulated.
32 devices in a mesh: row: 16 (over z, y, x), col: 2 (over core).
Axes of the slice: x: 2, y: 2, z: 4, core: 2. Of those that a mesh axis runs over, the one named last changes fastest.
Arguments:
- factor: bfloat16 [2, 2048, 65536], P(None, 'row', 'col'), may hold values from -40 to 40
- scales: float32 [2, 16, 512], P(None, 'row', 'col'), may hold values from 0 to 1, as said below
- coords: float32 [2, 2, 2048], replicated, may hold values from 0 to 1
- jitter: float32 [1], replicated, may hold values from 1 to 2
Outputs:
- new_columns: float32 [2, 2048, 256], P(None, ('row', 'col'))
Inputs may be any that keep to these rules, and one draw needn't show every extreme that they name: `scales`: positive.
All inputs are finite; a program needn't handle non-finite values.
Results may differ from a plain program's by a relative error of at most 0.0003.
Values may be sent and summed in bfloat16 or wider, within the bound.
A program may use at most 192 MiB of HBM per device.

v0:
```python
import jax
import jax.numpy as jnp
from jax import lax
from jax.sharding import PartitionSpec as P

PANEL = 128


SQRT_THREE = 1.7320508075688772
LENGTH_SCALE = 0.25


def broadcast(value, axis, root):
    mine = lax.axis_index(axis) == root
    return lax.psum(jnp.where(mine, value, jnp.zeros_like(value)), axis)


def matern(left_pts, right_pts):
    diff_x = left_pts[0][:, None] - right_pts[0][None, :]
    diff_y = left_pts[1][:, None] - right_pts[1][None, :]
    scaled = SQRT_THREE * jnp.sqrt(diff_x * diff_x + diff_y * diff_y) / LENGTH_SCALE
    return (1.0 + scaled) * jnp.exp(-scaled)


def right_solve(factor_low, values):
    return jax.scipy.linalg.solve_triangular(factor_low, values.T, lower=True).T


def on_device(factor, scales, coords, jitter):
    cycles, block_rows, width_local = factor.shape
    blocks_local = scales.shape[2]
    lead_width = 2 * PANEL
    widened = (
        factor.astype(jnp.float32).reshape(cycles, block_rows, blocks_local, PANEL)
        * scales[:, :, :, None]
    )
    dequant = widened.astype(jnp.bfloat16).reshape(cycles * block_rows, width_local)
    own_block = dequant[:PANEL]
    rows_one = broadcast(own_block, "row", 0)
    rows_two = broadcast(own_block, "row", 1)
    leading = jnp.concatenate([rows_one, rows_two], axis=0)
    products = lax.dot_general(
        dequant, leading, (((1,), (1,)), ((), ())), preferred_element_type=jnp.float32
    )
    row_index = lax.axis_index("row")
    col_index = lax.axis_index("col")
    row_count = lax.axis_size("row")
    col_count = lax.axis_size("col")
    share_rows = PANEL // col_count
    own_pts = lax.dynamic_slice_in_dim(coords, row_index * PANEL, PANEL, 2).reshape(
        2, cycles * PANEL
    )
    lead_pts = coords[:, 0, :lead_width]
    local_rows = jnp.arange(cycles * PANEL, dtype=jnp.int32)
    global_rows = local_rows // PANEL * (row_count * PANEL) + row_index * PANEL + local_rows % PANEL
    identity_mask = (
        global_rows[:, None] == jnp.arange(lead_width, dtype=jnp.int32)[None, :]
    ).astype(jnp.float32)
    kernel = matern(own_pts, lead_pts) + jitter[0] * identity_mask
    gram_part = lax.dot_general(
        leading, leading, (((1,), (1,)), ((), ())), preferred_element_type=jnp.float32
    )
    pieces = lax.psum_scatter(
        products.reshape(cycles, PANEL, lead_width), "col", scatter_dimension=1, tiled=True
    )
    gram_sum = lax.psum(gram_part.astype(jnp.bfloat16), "col").astype(jnp.float32)
    lead_kernel = matern(lead_pts, lead_pts) + jitter[0] * jnp.eye(lead_width, dtype=jnp.float32)
    factor_low = jnp.linalg.cholesky(lead_kernel - gram_sum)
    kernel_share = lax.dynamic_slice_in_dim(
        kernel.reshape(cycles, PANEL, lead_width), col_index * share_rows, share_rows, 1
    )
    window = (kernel_share - pieces).reshape(cycles * share_rows, lead_width)
    return right_solve(factor_low, window).reshape(cycles, share_rows, lead_width)


def solution(mesh):
    placed = (P(None, "row", "col"), P(None, "row", "col"), P(), P())
    return jax.shard_map(
        on_device,
        mesh=mesh,
        in_specs=placed,
        out_specs=P(None, ("row", "col"), None),
        check_vma=False,
    )
```

profile of v0, /device:TPU:29, one launch (start us, length us, event | category | flops | bytes accessed | tf_op | source)
XLA Modules:
  0.0 623.2 jit_solution(17977103327777877425)
XLA Ops:
  6.5 0.7 copy.31
  7.2 10.0 %copy.22 = f32[32,8,256,128]{3,2,1,0:T(8,128)S(1)} copy(bf16[32,8,256,128]{3,1,2,0:T(8,128)(2,1)} %bitcast.74) | data formatting | bytes 50331648
  17.2 6.2 broadcast_select_fusion
  23.4 20.1 %copy_bitcast_fusion = (bf16[128,32768]{1,0:T(8,128)(2,1)}, bf16[128,32768]{1,0:T(8,128)(2,1)}) fusion(bf16[16,8,256,128]{3,2,1,0:T(8,128)(2,1)} %bitcast.72, bf16[16,8,256,128]{3,2,1,0:T(8,128)(2,1)} %bitcast.73), kind=kLoop, calls=%fused_computation.8 | loop fusion | bytes 33554432 | tf_op jit(solution)/shard_map/jit(_where)/select_n | solution.py:15
  44.7 0.7 fusion.15
  45.4 0.7 fusion.19
  46.2 454.4 %all-reduce.7.cloned.1.call-done = (bf16[128,32768]{1,0:T(8,128)(2,1)}, bf16[128,32768]{1,0:T(8,128)(2,1)}) async-done(((bf16[128,32768]{1,0:T(8,128)(2,1)}, bf16[128,32768]{1,0:T(8,128)(2,1)}), (bf16[128,32768]{1,0:T(8,128)(2,1)}, bf16[128,32768]{1,0:T(8,128)(2,1)})) %all-reduce.7.cloned.1.call-update) | async-done | bytes 16777232 | tf_op jit(solution)/shard_map/psum | solution.py:15
  500.6 7.3 %constant_dynamic-update-slice_fusion.1 = bf16[256,32768]{1,0:T(8,128)(2,1)} fusion(bf16[128,32768]{1,0:T(8,128)(2,1)} %get-tuple-element.29), kind=kLoop, calls=%fused_computation.45 | loop fusion | bytes 16777216
  508.0 7.3 %constant_dynamic-update-slice_fusion = bf16[256,32768]{1,0:T(8,128)(2,1)} fusion(bf16[256,32768]{1,0:T(8,128)(2,1)} %constant_dynamic-update-slice_fusion.1, bf16[128,32768]{1,0:T(8,128)(2,1)} %get-tuple-element.30), kind=kLoop, calls=%fused_computation.44 | loop fusion | bytes 16777216 | tf_op jit(solution)/shard_map/concatenate | solution.py:41
  515.3 15.7 %convolution_convert_fusion = bf16[256,256]{0,1:T(8,128)(2,1)} fusion(bf16[256,32768]{1,0:T(8,128)(2,1)} %constant_dynamic-update-slice_fusion), kind=kOutput, calls=%fused_computation.13 | convolution fusion | flops 4295032832 | bytes 16908288 | tf_op jit(solution)/shard_map/dot_general | solution.py:60
  531.0 0.2 reduce-scatter.2.cloned.1.call-start
  531.3 13.7 %fusion = f32[2,128,256]{2,1,0:T(8,128)} fusion(bf16[256,32768]{1,0:T(8,128)(2,1)} %constant_dynamic-update-slice_fusion, f32[2,32768]{1,0:T(2,128)S(1)} %bitcast.77, bf16[2,128,32768]{2,1,0:T(8,128)(2,1)} %param.4), kind=kOutput, calls=%fused_computation.3 | convolution fusion | flops 4320133120 | bytes 34078720 | tf_op jit(solution)/shard_map/dot_general | solution.py:42
  545.0 5.5 all-reduce.5.cloned.1.call-done
  550.5 1.2 convert_subtract_fusion
  551.8 1.2 fusion.5
  553.0 11.7 %cholesky.49 = f32[128,128]{1,0:T(8,128)S(1)} custom-call(f32[128,128]{1,0:T(8,128)S(1)} %cholesky.115), custom_call_target="Cholesky" | custom-call | tf_op jit(solution)/shard_map/jit(cholesky)/cholesky | solution.py:68
  564.8 9.8 %custom-call.15 = f32[1,128,128]{1,2,0:T(8,128)S(1)} custom-call(f32[1,128,128]{2,1,0:T(8,128)S(1)} %get-tuple-element.36), custom_call_target="InvertDiagBlocksLowerTriangular" | custom-call | tf_op jit(solution)/shard_map/jit(cholesky)/cholesky | solution.py:68
  574.8 0.3 convolution_subtract_fusion.1
  575.1 11.7 %cholesky.103 = f32[128,128]{1,0:T(8,128)S(1)} custom-call(f32[128,128]{1,0:T(8,128)S(1)} %convolution_subtract_fusion.1), custom_call_target="Cholesky" | custom-call | tf_op jit(solution)/shard_map/jit(cholesky)/cholesky | solution.py:68
  587.1 0.7 compare_reduce_fusion
  587.8 0.6 compare_reduce_fusion.1
  589.9 4.2 while.1
  589.9 0.6 fusion.27
  590.5 1.4 dynamic-slice.17
  592.0 0.6 fusion.27
  592.6 1.4 dynamic-slice.17
  594.1 19.9 %custom-call.16 = f32[2,128,128]{1,2,0:T(8,128)S(1)} custom-call(f32[2,128,128]{2,1,0:T(8,128)S(1)} %get-tuple-element.12), custom_call_target="InvertDiagBlocksLowerTriangular" | custom-call | tf_op jit(solution)/shard_map/jit(_solve_triangular)/triangular_solve | solution.py:26
  614.0 1.0 add_subtract_fusion
  615.0 0.3 fusion.9
  615.3 0.3 convolution_subtract_fusion
  615.6 0.3 fusion.8
  615.9 0.8 copy.18
  (34 shorter events, 1.7 us)
Async XLA Ops:
  6.5 494.1 %all-reduce.7.cloned.1.call-start = ((), (), s32[]{:S(2)}) async-start(), calls=%async_computation.3 | async-start | bytes 33554432 | tf_op jit(solution)/shard_map/psum | solution.py:15
  43.5 507.0 %all-reduce.5.cloned.1.call-start = ((), (), s32[]{:S(2)}) async-start(), calls=%async_computation.1 | async-start | bytes 262144 | tf_op jit(solution)/shard_map/psum | solution.py:66
  531.0 83.0 %reduce-scatter.2.cloned.1.call-start = ((), (), s32[]{:S(2)}) async-start(), calls=%async_computation.2 | async-start | bytes 393216 | tf_op jit(solution)/shard_map/reduce_scatter | solution.py:63
Sparse Core Ops, SparseCore 0:
  43.7 456.9 all-reduce.6
  531.2 19.3 all-reduce.4
  552.8 8.8 reduce-scatter.1
where the time goes:
time: 625 us; the launch traced here: 623 us
  waiting for transfers between devices  460 us (74%)
  other arithmetic  64.2 us (10%)
  local copies, waits for them, and re-layouts  52.7 us (8%)
  matrix products  30.7 us (5%)
  between operations  15.3 us (2%)
    psum x1, waiting for transfers between devices, broadcast(): return lax.psum(jnp.where(mine, value, jnp.zeros_like(value)), axis)  454 us
    another operation x7, other arithmetic, on_device(): factor_low = jnp.linalg.cholesky(lead_kernel - gram_sum)  34.6 us
    select_n x1, local copies, waits for them, and re-layouts, broadcast(): return lax.psum(jnp.where(mine, value, jnp.zeros_like(value)), axis)  20.1 us
    another operation x3, other arithmetic, right_solve(): return jax.scipy.linalg.solve_triangular(factor_low, values.T, lower=True).T  19.9 us
    unnamed x5, local copies, waits for them, and re-layouts  18.3 us
    dot_general x1, matrix products, on_device(): lax.dot_general(leading, leading, (((1,), (1,)), ((), ())), preferred_ele...  15.7 us
    dot_general x1, matrix products, on_device(): lax.dot_general(dequant, leading, (((1,), (1,)), ((), ())), preferred_ele...  13.7 us
  transfers between devices with their start and end apart: 3, of which 2 were waited for; matrix products, arithmetic and copies ran while one was open for 12% of the time, Pallas kernels for 0%

commit v1 on v0

v1 whole, which is shorter than its diff:
```python
import functools
import jax
import jax.numpy as jnp
from jax import lax
from jax.experimental import pallas as pl
from jax.experimental.pallas import tpu as pltpu
from jax.sharding import PartitionSpec as P

PANEL = 128
CHUNK = 256
SKEW = 2
HEAD = 8

SQRT_THREE = 1.7320508075688772
LENGTH_SCALE = 0.25
MESH = pl.DeviceIdType.MESH
TREES = 3
TWIN, CHAIN, LIFT = 0, 2, 1


def matern(left_pts, right_pts):
    diff_x = left_pts[0][:, None] - right_pts[0][None, :]
    diff_y = left_pts[1][:, None] - right_pts[1][None, :]
    scaled = SQRT_THREE * jnp.sqrt(diff_x * diff_x + diff_y * diff_y) / LENGTH_SCALE
    return (1.0 + scaled) * jnp.exp(-scaled)


def right_solve(factor_low, values):
    return jax.scipy.linalg.solve_triangular(factor_low, values.T, lower=True).T


def counts_of(chunks):
    return [chunks // TREES + (1 if t < chunks % TREES else 0) for t in range(TREES)]


def roles(tree, xs, y, z, planes):
    top = z == planes - 1
    low = z == 0
    a = (xs == 0) & (y == 0)
    b = (xs == 1) & (y == 0)
    c = (xs == 1) & (y == 1)
    d = (xs == 0) & (y == 1)
    up = jnp.logical_not(top)
    if tree == TWIN:
        return z + y + xs, xs == 0, a & low, (xs == 0) & up, None
    high = jnp.logical_not(low)
    if tree == CHAIN:
        place = jnp.where(d, 1, jnp.where(a, 2, jnp.where(b, 3, 4)))
        depth = jnp.where(low, xs + y, z + place)
        send_x = (low & (xs == 0)) | (high & a)
        send_y = (low & a) | (high & (d | b))
        return depth, send_x, send_y, d & up, None
    place = jnp.where(a, 0, jnp.where(d, 1, jnp.where(c, 2, 3)))
    depth = jnp.where(low, jnp.where(a, 0, place + 2), z + place)
    return depth, high & d, high & (a | c), a & up, (z == 1) & jnp.logical_not(a)


def gather_products(rows, factor_hbm, scales_ref, prod_ref, gram_ref,
                    raw, lead, lhs, acc, got_prod, got_gram,
                    load_sem, send_sem, recv_sem, swap_sem):
    cycles, _, width = raw.shape
    row = lax.axis_index("row")
    col = lax.axis_index("col")
    chunks = width // CHUNK
    counts = counts_of(chunks)
    starts = [sum(counts[:t]) for t in range(TREES)]
    planes = rows // 4
    x = row % 2
    y = (row // 2) % 2
    z = row // 4
    targets = [
        row + 1 - 2 * x,
        row + 2 - 4 * y,
        jnp.minimum(row + 4, rows - 1),
        jnp.maximum(row - 4, 0),
    ]
    has_up = z < planes - 1
    has_down = z > 0
    partner = 1 - col

    head = min(HEAD, min(counts) - 1)
    loads = []
    for t in range(TREES):
        for part, (low, size) in enumerate(((0, head), (head, counts[t] - head))):
            span = pl.ds((starts[t] + low) * CHUNK, size * CHUNK)
            loads.append(pltpu.make_async_copy(
                factor_hbm.at[:, :, span], raw.at[:, :, span], load_sem.at[t, part]))
    for t in range(TREES):
        loads[2 * t].start()
    for t in range(TREES):
        loads[2 * t + 1].start()

    barrier = pltpu.get_barrier_semaphore()

    def greet(target):
        pl.semaphore_signal(barrier, inc=1, device_id=target, device_id_type=MESH)

    greet((targets[0], col))
    greet((targets[1], col))
    greet((row, partner))
    pl.when(has_up)(lambda: greet((targets[2], col)))
    pl.when(has_down)(lambda: greet((targets[3], col)))
    acc[...] = jnp.zeros_like(acc)
    pl.semaphore_wait(barrier, 3 + has_up.astype(jnp.int32) + has_down.astype(jnp.int32))

    depths = [[None] * TREES for _ in range(2)]
    sends = [[None] * TREES for _ in range(2)]
    for s in range(2):
        xs = x if s == 0 else 1 - x
        for t in range(TREES):
            depth, *send = roles(t, xs, y, z, planes)
            depths[s][t] = depth
            sends[s][t] = send
    last = planes - 1 + 4

    def piece(s, t, index, size=1):
        return lead.at[s, :, pl.ds(pl.multiple_of((starts[t] + index) * CHUNK, CHUNK), size * CHUNK)]

    def dequantize(cycle, chunk, out, out_row, out_at):
        for b in range(CHUNK // PANEL):
            at = pl.multiple_of(chunk * CHUNK + b * PANEL, PANEL)
            scale = scales_ref[cycle, chunk * (CHUNK // PANEL) + b]
            block = raw[cycle, :, pl.ds(at, PANEL)].astype(jnp.float32) * scale
            out(b, block.astype(jnp.bfloat16))

    def forward(s, t, step):
        index = step - SKEW * depths[s][t]

        @pl.when((index >= 0) & (index < counts[t]))
        def _():
            here = piece(s, t, index)

            @pl.when(row == s)
            def _():
                def put(b, block):
                    at = pl.multiple_of((starts[t] + index) * CHUNK + b * PANEL, PANEL)
                    lead[s, :, pl.ds(at, PANEL)] = block
                dequantize(0, starts[t] + index, put, 0, 0)

            @pl.when(row != s)
            def _():
                pltpu.make_async_copy(here, here, recv_sem.at[s, t, index]).wait()

            for way in range(4):
                wanted = sends[s][t][way]
                if wanted is None:
                    continue

                @pl.when(wanted)
                def _():
                    pltpu.make_async_remote_copy(
                        src_ref=here, dst_ref=here,
                        send_sem=send_sem.at[s, t, way], recv_sem=recv_sem.at[s, t, index],
                        device_id=(targets[way], col), device_id_type=MESH,
                    ).start()

    def multiply(t, step):
        index = step - SKEW * jnp.maximum(depths[0][t], depths[1][t])

        @pl.when((index >= 0) & (index < counts[t]))
        def _():
            chunk = starts[t] + index
            for cycle in range(cycles):
                def put(b, block):
                    lhs[cycle * PANEL:(cycle + 1) * PANEL, b * PANEL:(b + 1) * PANEL] = block
                dequantize(cycle, chunk, put, 0, 0)
            span = pl.ds(pl.multiple_of(chunk * CHUNK, CHUNK), CHUNK)
            right = lead[:, :, span].reshape(2 * PANEL, CHUNK)
            own = lhs[...]
            dims = (((1,), (1,)), ((), ()))
            top = cycles * PANEL
            acc[:top] += lax.dot_general(own, right, dims, preferred_element_type=jnp.float32)
            acc[top:] += lax.dot_general(right, right, dims, preferred_element_type=jnp.float32)

    def one_step(step, carry):
        for t in range(TREES):
            for s in range(2):
                forward(s, t, step)
        for t in range(TREES):
            multiply(t, step)
        return carry

    for t in range(TREES):
        loads[2 * t].wait()
    lax.fori_loop(0, head, one_step, 0)
    for t in range(TREES):
        loads[2 * t + 1].wait()
    lax.fori_loop(head, max(counts) + SKEW * last, one_step, 0)

    share = PANEL // 2
    top = cycles * PANEL
    swaps = []
    for cycle in range(cycles):
        at = pl.multiple_of(cycle * PANEL + partner * share, share)
        swaps.append((acc.at[pl.ds(at, share)], got_prod.at[cycle]))
    swaps.append((acc.at[pl.ds(top, 2 * PANEL)], got_gram))
    copies = []
    for k, (source, target) in enumerate(swaps):
        copies.append(pltpu.make_async_remote_copy(
            src_ref=source, dst_ref=target, send_sem=swap_sem.at[0, k], recv_sem=swap_sem.at[1, k],
            device_id=(row, partner), device_id_type=MESH))
    for copy in copies:
        copy.start()
    for s in range(2):
        for t in range(TREES):
            for way in range(4):
                wanted = sends[s][t][way]
                if wanted is None:
                    continue

                @pl.when(wanted)
                def _():
                    whole = piece(s, t, 0, counts[t])
                    pltpu.make_async_remote_copy(
                        src_ref=whole, dst_ref=whole,
                        send_sem=send_sem.at[s, t, way], recv_sem=recv_sem.at[s, t, 0],
                        device_id=(targets[way], col), device_id_type=MESH,
                    ).wait_send()
    for copy in copies:
        copy.wait()
    for cycle in range(cycles):
        at = pl.multiple_of(cycle * PANEL + col * share, share)
        prod_ref[cycle] = acc[pl.ds(at, share)] + got_prod[cycle]
    gram_ref[...] = acc[top:] + got_gram[...]


def on_device(rows, factor, scales, coords, jitter):
    cycles, block_rows, width_local = factor.shape
    lead_width = 2 * PANEL
    col_count = lax.axis_size("col")
    share_rows = PANEL // col_count
    chunks = width_local // CHUNK
    pieces, gram_sum = pl.pallas_call(
        functools.partial(gather_products, rows),
        out_shape=(
            jax.ShapeDtypeStruct((cycles, share_rows, lead_width), jnp.float32),
            jax.ShapeDtypeStruct((lead_width, lead_width), jnp.float32),
        ),
        in_specs=[
            pl.BlockSpec(memory_space=pl.ANY),
            pl.BlockSpec(memory_space=pltpu.SMEM),
        ],
        out_specs=(
            pl.BlockSpec(memory_space=pltpu.VMEM),
            pl.BlockSpec(memory_space=pltpu.VMEM),
        ),
        scratch_shapes=[
            pltpu.VMEM((cycles, PANEL, width_local), jnp.bfloat16),
            pltpu.VMEM((2, PANEL, width_local), jnp.bfloat16),
            pltpu.VMEM((cycles * PANEL, CHUNK), jnp.bfloat16),
            pltpu.VMEM((cycles * PANEL + lead_width, lead_width), jnp.float32),
            pltpu.VMEM((cycles, share_rows, lead_width), jnp.float32),
            pltpu.VMEM((lead_width, lead_width), jnp.float32),
            pltpu.SemaphoreType.DMA((TREES, 2)),
            pltpu.SemaphoreType.DMA((2, TREES, 4)),
            pltpu.SemaphoreType.DMA((2, TREES, max(counts_of(chunks)))),
            pltpu.SemaphoreType.DMA((2, cycles + 1)),
        ],
        compiler_params=pltpu.CompilerParams(
            collective_id=0, has_side_effects=True, vmem_limit_bytes=48 * 1024 * 1024),
        cost_estimate=pl.CostEstimate(
            flops=8 * cycles * PANEL * lead_width * width_local,
            bytes_accessed=factor.size * 2, transcendentals=0),
        name="gather_products",
    )(factor, scales.reshape(cycles, -1))
    row_index = lax.axis_index("row")
    col_index = lax.axis_index("col")
    row_count = lax.axis_size("row")
    own_pts = lax.dynamic_slice_in_dim(
        coords, row_index * PANEL + col_index * share_rows, share_rows, 2
    ).reshape(2, cycles * share_rows)
    lead_pts = coords[:, 0, :lead_width]
    local_rows = jnp.arange(cycles * share_rows, dtype=jnp.int32)
    global_rows = (
        local_rows // share_rows * (row_count * PANEL)
        + row_index * PANEL + col_index * share_rows + local_rows % share_rows
    )
    identity_mask = (
        global_rows[:, None] == jnp.arange(lead_width, dtype=jnp.int32)[None, :]
    ).astype(jnp.float32)
    kernel = matern(own_pts, lead_pts) + jitter[0] * identity_mask
    lead_kernel = matern(lead_pts, lead_pts) + jitter[0] * jnp.eye(lead_width, dtype=jnp.float32)
    factor_low = jnp.linalg.cholesky(lead_kernel - gram_sum)
    window = kernel - pieces.reshape(cycles * share_rows, lead_width)
    return right_solve(factor_low, window).reshape(cycles, share_rows, lead_width)


def solution(mesh):
    placed = (P(None, "row", "col"), P(None, "row", "col"), P(), P())
    return jax.shard_map(
        functools.partial(on_device, mesh.shape["row"]),
        mesh=mesh,
        in_specs=placed,
        out_specs=P(None, ("row", "col"), None),
        check_vma=False,
    )
```

time: 625 us -> 215 us (0.34)
  waiting for transfers between devices: 460 us -> 0 us
  Pallas kernels: 0 us -> 149 us
  local copies, waits for them, and re-layouts: 52.7 us -> 7.94 us
  matrix products: 30.7 us -> 1.33 us
  between operations: 15.3 us -> 2.11 us
  other arithmetic: 64.2 us -> 54.6 us
    psum x2 -> x0, waiting for transfers between devices: 460 us -> none  [the longest x1 454 us: broadcast(): return lax.psum(jnp.where(mine, value, jnp.zeros_like(value)), axis)]
    pallas_call x0 -> x1, Pallas kernels: none -> 149 us  [on_device(): pl.pallas_call(functools.partial(gather_products, rows), out_shape=(jax.S...]
    dot_general x2 -> x0, matrix products: 29.4 us -> none  [the longest x1 15.7 us: on_device(): lax.dot_general(leading, leading, (((1,), (1,)), ((), ())), preferred_ele...]
    select_n x1 -> x0, local copies, waits for them, and re-layouts: 20.1 us -> none  [broadcast(): return lax.psum(jnp.where(mine, value, jnp.zeros_like(value)), axis)]
    unnamed x5 -> x1, local copies, waits for them, and re-layouts: 18.3 us -> 0.68 us
    concatenate x1 -> x0, local copies, waits for them, and re-layouts: 7.33 us -> none  [on_device(): leading = jnp.concatenate([rows_one, rows_two], axis=0)]
    another operation x7 -> x6, other arithmetic: 34.6 us -> 34 us  [on_device(): factor_low = jnp.linalg.cholesky(lead_kernel - gram_sum)]
  transfers between devices with their start and end apart: 3 -> 0, of which waited for: 2 -> 0; matrix products, arithmetic and copies ran while one was open for 12% -> 0% of each run, Pallas kernels for 0% -> 0%
where the time goes in v1:
time: 215 us
  Pallas kernels  149 us (69%)
  other arithmetic  54.6 us (25%)
  local copies, waits for them, and re-layouts  7.94 us (4%)
    pallas_call x1, Pallas kernels, on_device(): pl.pallas_call(functools.partial(gather_products, rows), out_shape=(jax.S...  149 us
    another operation x6, other arithmetic, on_device(): factor_low = jnp.linalg.cholesky(lead_kernel - gram_sum)  34 us
    another operation x3, other arithmetic, right_solve(): return jax.scipy.linalg.solve_triangular(factor_low, values.T, lower=True).T  19.9 us

profile of v1, /device:TPU:29, one launch (start us, length us, event | category | flops | bytes accessed | tf_op | source)
XLA Modules:
  0.0 215.0 jit_solution(950472996090493717)
XLA Ops:
  0.0 0.7 fusion.13
  0.7 0.7 copy.22
  1.4 148.9 %gather_products.1 = (f32[2,64,256]{2,1,0:T(8,128)S(1)}, f32[256,256]{1,0:T(8,128)S(1)}) custom-call(bf16[2,128,32768]{2,1,0:T(8,128)(2,1)} %factor_hbm.1, f32[2,256]{1,0:T(2,128)S(1)} %bitcast.44), custom_call_target="tpu_custom_call" | custom-call | flops 17179869184 | bytes 16777216 | tf_op jit(solution)/shard_map/gather_products/pallas_call | solution.py:233
  150.3 0.1 copy.12
  151.1 0.2 add_subtract_fusion
  151.4 0.1 copy.13
  151.5 0.3 fusion
  151.8 11.7 %cholesky.50 = f32[128,128]{1,0:T(8,128)S(1)} custom-call(f32[128,128]{1,0:T(8,128)S(1)} %cholesky.118), custom_call_target="Cholesky" | custom-call | tf_op jit(solution)/shard_map/jit(cholesky)/cholesky | solution.py:283
  163.6 9.8 %custom-call.15 = f32[1,128,128]{1,2,0:T(8,128)S(1)} custom-call(f32[1,128,128]{2,1,0:T(8,128)S(1)} %get-tuple-element.36), custom_call_target="InvertDiagBlocksLowerTriangular" | custom-call | tf_op jit(solution)/shard_map/jit(cholesky)/cholesky | solution.py:283
  173.4 0.2 fusion.5
  173.6 0.3 convolution_subtract_fusion.1
  173.8 11.7 %cholesky.105 = f32[128,128]{1,0:T(8,128)S(1)} custom-call(f32[128,128]{1,0:T(8,128)S(1)} %convolution_subtract_fusion.1), custom_call_target="Cholesky" | custom-call | tf_op jit(solution)/shard_map/jit(cholesky)/cholesky | solution.py:283
  185.6 0.7 compare_reduce_fusion
  187.6 0.1 copy.16
  187.7 0.1 copy.15
  187.8 0.1 copy.14
  188.1 4.3 %while.1 = (s32[]{:T(128)}, f32[256,256]{0,1:T(8,128)S(1)}, s32[2,2]{1,0:T(2,128)S(1)}, f32[2,128,128]{2,1,0:T(8,128)S(1)}, s32[]{:T(128)}) while((s32[]{:T(128)}, f32[256,256]{0,1:T(8,128)S(1)}, s32[2,2]{1,0:T(2,128)S(1)}, f32[2,128,128]{2,1,0:T(8,128)S(1)}, s32[]{:T(128)}) %tuple.25), condition=%wide.while_cond, body=%wide.while_body.sunk | while | flops 2 | bytes 393321 | solution.py:29
  188.1 0.7 fusion.19
  188.7 1.3 dynamic-slice.11
  190.1 0.1 copy.24
  190.2 0.7 fusion.19
  190.9 1.3 dynamic-slice.11
  192.2 0.1 copy.24
  192.4 19.9 %custom-call.16 = f32[2,128,128]{1,2,0:T(8,128)S(1)} custom-call(f32[2,128,128]{2,1,0:T(8,128)S(1)} %get-tuple-element.16), custom_call_target="InvertDiagBlocksLowerTriangular" | custom-call | tf_op jit(solution)/shard_map/jit(_solve_triangular)/triangular_solve | solution.py:29
  212.2 0.8 constant_dynamic-slice_fusion.1
  213.0 0.1 sub.81
  213.1 0.1 sub.85
  213.2 0.2 bitcast_subtract_fusion
  213.4 0.3 fusion.3
  213.6 0.3 convolution_subtract_fusion
  213.9 0.3 fusion.2
  214.3 0.8 copy.18
  (16 shorter events, 0.3 us)

commit v2 on v1

--- a/solution.py
+++ b/solution.py
@@ -7,9 +7,10 @@
 from jax.sharding import PartitionSpec as P
 
 PANEL = 128
-CHUNK = 256
+CHUNK = 128
+PAIR = 2
 SKEW = 2
-HEAD = 8
+HEAD = 16
 
 SQRT_THREE = 1.7320508075688772
 LENGTH_SCALE = 0.25
@@ -25,12 +26,58 @@
     return (1.0 + scaled) * jnp.exp(-scaled)
 
 
-def right_solve(factor_low, values):
-    return jax.scipy.linalg.solve_triangular(factor_low, values.T, lower=True).T
+def exact_dot(left, right, transposed):
+    dims = (((1,), (1 if transposed else 0,)), ((), ()))
+    return lax.dot_general(
+        left, right, dims, precision=lax.Precision.HIGHEST, preferred_element_type=jnp.float32
+    )
+
+
+def inverse_factor(block, out_ref):
+    size = block.shape[0]
+    tiles = size // 8
+    sub = lax.broadcasted_iota(jnp.int32, (8, size), 0)
+    lane = lax.broadcasted_iota(jnp.int32, (8, size), 1)
+    left = [block[8 * k:8 * k + 8] for k in range(tiles)]
+    right = [(lane == sub + 8 * k).astype(jnp.float32) for k in range(tiles)]
+    for j in range(size):
+        home, r = j // 8, j % 8
+        row_left = left[home][r:r + 1, :]
+        row_right = right[home][r:r + 1, :]
+        pivot = jnp.broadcast_to(row_left[:, j:j + 1], (1, size))
+        out_ref[j:j + 1, :] = row_right * lax.rsqrt(pivot)
+        if j == size - 1:
+            break
+        inverse = 1.0 / pivot
+        scaled_left = row_left * inverse
+        scaled_right = row_right * inverse
+        for k in range(home, tiles):
+            if k == home and r == 7:
+                continue
+            column = jnp.broadcast_to(left[k][:, j:j + 1], (8, size))
+            if k == home:
+                column = jnp.where(sub > r, column, 0.0)
+            left[k] = left[k] - column * scaled_left
+            right[k] = right[k] - column * scaled_right
+
+
+def solve_panels(gram_ref, lead_ref, prod_ref, kernel_ref, out_ref, block, inv_one, inv_two):
+    half = block.shape[0]
+    block[...] = lead_ref[:half, :half] - gram_ref[:half, :half]
+    inverse_factor(block[...], inv_one)
+    first = inv_one[...]
+    below = exact_dot(lead_ref[half:, :half] - gram_ref[half:, :half], first, True)
+    block[...] = lead_ref[half:, half:] - gram_ref[half:, half:] - exact_dot(below, below, True)
+    one = exact_dot(kernel_ref[:, :half] - prod_ref[:, :half], first, True)
+    rest = kernel_ref[:, half:] - prod_ref[:, half:] - exact_dot(one, below, True)
+    inverse_factor(block[...], inv_two)
+    out_ref[:, :half] = one
+    out_ref[:, half:] = exact_dot(rest, inv_two[...], True)
 
 
 def counts_of(chunks):
-    return [chunks // TREES + (1 if t < chunks % TREES else 0) for t in range(TREES)]
+    pairs = chunks // PAIR
+    return [PAIR * (pairs // TREES + (1 if t < pairs % TREES else 0)) for t in range(TREES)]
 
 
 def roles(tree, xs, y, z, planes):
@@ -78,7 +125,7 @@
     has_down = z > 0
     partner = 1 - col
 
-    head = min(HEAD, min(counts) - 1)
+    head = min(HEAD, min(counts) - PAIR)
     loads = []
     for t in range(TREES):
         for part, (low, size) in enumerate(((0, head), (head, counts[t] - head))):
@@ -114,14 +161,12 @@
     last = planes - 1 + 4
 
     def piece(s, t, index, size=1):
-        return lead.at[s, :, pl.ds(pl.multiple_of((starts[t] + index) * CHUNK, CHUNK), size * CHUNK)]
-
-    def dequantize(cycle, chunk, out, out_row, out_at):
-        for b in range(CHUNK // PANEL):
-            at = pl.multiple_of(chunk * CHUNK + b * PANEL, PANEL)
-            scale = scales_ref[cycle, chunk * (CHUNK // PANEL) + b]
-            block = raw[cycle, :, pl.ds(at, PANEL)].astype(jnp.float32) * scale
-            out(b, block.astype(jnp.bfloat16))
+        return lead.at[s, pl.ds(starts[t] + index, size)]
+
+    def dequantize(cycle, chunk):
+        at = pl.multiple_of(chunk * CHUNK, CHUNK)
+        block = raw[cycle, :, pl.ds(at, CHUNK)].astype(jnp.float32) * scales_ref[cycle, chunk]
+        return block.astype(jnp.bfloat16)
 
     def forward(s, t, step):
         index = step - SKEW * depths[s][t]
@@ -132,10 +177,7 @@
 
             @pl.when(row == s)
             def _():
-                def put(b, block):
-                    at = pl.multiple_of((starts[t] + index) * CHUNK + b * PANEL, PANEL)
-                    lead[s, :, pl.ds(at, PANEL)] = block
-                dequantize(0, starts[t] + index, put, 0, 0)
+                lead[s, starts[t] + index] = dequantize(0, starts[t] + index)
 
             @pl.when(row != s)
             def _():
@@ -157,15 +199,16 @@
     def multiply(t, step):
         index = step - SKEW * jnp.maximum(depths[0][t], depths[1][t])
 
-        @pl.when((index >= 0) & (index < counts[t]))
+        @pl.when((index >= 0) & (index < counts[t]) & (index % PAIR == PAIR - 1))
         def _():
-            chunk = starts[t] + index
+            first = starts[t] + index - (PAIR - 1)
             for cycle in range(cycles):
-                def put(b, block):
-                    lhs[cycle * PANEL:(cycle + 1) * PANEL, b * PANEL:(b + 1) * PANEL] = block
-                dequantize(cycle, chunk, put, 0, 0)
-            span = pl.ds(pl.multiple_of(chunk * CHUNK, CHUNK), CHUNK)
-            right = lead[:, :, span].reshape(2 * PANEL, CHUNK)
+                for b in range(PAIR):
+                    lhs[cycle * PANEL:(cycle + 1) * PANEL, b * CHUNK:(b + 1) * CHUNK] = (
+                        dequantize(cycle, first + b))
+            right = jnp.concatenate([
+                jnp.concatenate([lead[s, first + b] for b in range(PAIR)], axis=1)
+                for s in range(2)], axis=0)
             own = lhs[...]
             dims = (((1,), (1,)), ((), ()))
             top = cycles * PANEL
@@ -246,8 +289,8 @@
         ),
         scratch_shapes=[
             pltpu.VMEM((cycles, PANEL, width_local), jnp.bfloat16),
-            pltpu.VMEM((2, PANEL, width_local), jnp.bfloat16),
-            pltpu.VMEM((cycles * PANEL, CHUNK), jnp.bfloat16),
+            pltpu.VMEM((2, chunks, PANEL, CHUNK), jnp.bfloat16),
+            pltpu.VMEM((cycles * PANEL, PAIR * CHUNK), jnp.bfloat16),
             pltpu.VMEM((cycles * PANEL + lead_width, lead_width), jnp.float32),
             pltpu.VMEM((cycles, share_rows, lead_width), jnp.float32),
             pltpu.VMEM((lead_width, lead_width), jnp.float32),
@@ -280,9 +323,14 @@
     ).astype(jnp.float32)
     kernel = matern(own_pts, lead_pts) + jitter[0] * identity_mask
     lead_kernel = matern(lead_pts, lead_pts) + jitter[0] * jnp.eye(lead_width, dtype=jnp.float32)
-    factor_low = jnp.linalg.cholesky(lead_kernel - gram_sum)
-    window = kernel - pieces.reshape(cycles * share_rows, lead_width)
-    return right_solve(factor_low, window).reshape(cycles, share_rows, lead_width)
+    solved = pl.pallas_call(
+        solve_panels,
+        out_shape=jax.ShapeDtypeStruct((cycles * share_rows, lead_width), jnp.float32),
+        scratch_shapes=[pltpu.VMEM((PANEL, PANEL), jnp.float32)] * 3,
+        compiler_params=pltpu.CompilerParams(vmem_limit_bytes=16 * 1024 * 1024),
+        name="solve_panels",
+    )(gram_sum, lead_kernel, pieces.reshape(cycles * share_rows, lead_width), kernel)
+    return solved.reshape(cycles, share_rows, lead_width)
 
 
 def solution(mesh):

time: 215 us -> 191 us (0.89)
  other arithmetic: 54.6 us -> 0.41 us
  Pallas kernels: 149 us -> 187 us
  local copies, waits for them, and re-layouts: 7.94 us -> 2.32 us
    another operation x9 -> x0, other arithmetic: 53.9 us -> none  [the longest x6 34 us: on_device(): factor_low = jnp.linalg.cholesky(lead_kernel - gram_sum)]
    pallas_call x0 -> x1, Pallas kernels: none -> 22.9 us  [on_device(): pl.pallas_call(solve_panels, out_shape=jax.ShapeDtypeStruct((cycles * sha...]
    pallas_call x1, Pallas kernels: 149 us -> 164 us  [on_device(): pl.pallas_call(functools.partial(gather_products, rows), out_shape=(jax.S...]
    another operation x18 -> x0, local copies, waits for them, and re-layouts: 4.61 us -> none
where the time goes in v2:
time: 191 us
  Pallas kernels  187 us (98%)
  local copies, waits for them, and re-layouts  2.32 us (1%)
    pallas_call x1, Pallas kernels, on_device(): pl.pallas_call(functools.partial(gather_products, rows), out_shape=(jax.S...  164 us
    pallas_call x1, Pallas kernels, on_device(): pl.pallas_call(solve_panels, out_shape=jax.ShapeDtypeStruct((cycles * sha...  22.9 us

profile of v2, /device:TPU:29, one launch (start us, length us, event | category | flops | bytes accessed | tf_op | source)
XLA Modules:
  0.0 190.6 jit_solution(16403376728884929526)
XLA Ops:
  0.7 0.8 constant_dynamic-slice_fusion
  1.4 0.1 sub.74
  1.5 0.1 sub.78
  1.6 0.7 copy.7
  2.3 0.7 fusion.4
  3.0 0.2 select_add_fusion.1.kernel_ref
  3.2 0.2 select_add_fusion.lead_ref
  3.4 164.2 %gather_products.1 = (f32[2,64,256]{2,1,0:T(8,128)S(1)}, f32[256,256]{1,0:T(8,128)S(1)}) custom-call(bf16[2,128,32768]{2,1,0:T(8,128)(2,1)} %factor_hbm.1, f32[2,256]{1,0:T(2,128)S(1)} %bitcast.11), custom_call_target="tpu_custom_call" | custom-call | flops 17179869184 | bytes 16777216 | tf_op jit(solution)/shard_map/gather_products/pallas_call | solution.py:276
  167.7 22.9 %solve_panels.1 = f32[128,256]{1,0:T(8,128)} custom-call(f32[256,256]{1,0:T(8,128)S(1)} %get-tuple-element.7.gram_ref, f32[256,256]{1,0:T(8,128)S(1)} %select_add_fusion.lead_ref, f32[128,256]{1,0:T(8,128)S(1)} %bitcast.10, f32[128,256]{1,0:T(8,128)S(1)} %select_add_fusion.1.kernel_ref), custom_call_target="tpu_custom_call" | custom-call | tf_op jit(solution)/shard_map/solve_panels/pallas_call | solution.py:326
  (1 shorter events, 0.0 us)

commit v3 on v2

--- a/solution.py
+++ b/solution.py
@@ -8,7 +8,7 @@
 
 PANEL = 128
 CHUNK = 128
-PAIR = 2
+GROUP = 4
 SKEW = 2
 HEAD = 16
 
@@ -40,25 +40,36 @@
     lane = lax.broadcasted_iota(jnp.int32, (8, size), 1)
     left = [block[8 * k:8 * k + 8] for k in range(tiles)]
     right = [(lane == sub + 8 * k).astype(jnp.float32) for k in range(tiles)]
-    for j in range(size):
+    for j in range(0, size, 2):
         home, r = j // 8, j % 8
-        row_left = left[home][r:r + 1, :]
-        row_right = right[home][r:r + 1, :]
-        pivot = jnp.broadcast_to(row_left[:, j:j + 1], (1, size))
-        out_ref[j:j + 1, :] = row_right * lax.rsqrt(pivot)
-        if j == size - 1:
+        left_one, left_two = left[home][r:r + 1, :], left[home][r + 1:r + 2, :]
+        right_one, right_two = right[home][r:r + 1, :], right[home][r + 1:r + 2, :]
+        first = jnp.broadcast_to(left_one[:, j:j + 1], (1, size))
+        cross = jnp.broadcast_to(left_one[:, j + 1:j + 2], (1, size))
+        second = jnp.broadcast_to(left_two[:, j + 1:j + 2], (1, size))
+        det = first * second - cross * cross
+        lower = first * right_two - cross * right_one
+        out_ref[j:j + 1, :] = right_one * lax.rsqrt(first)
+        out_ref[j + 1:j + 2, :] = lower * lax.rsqrt(first * det)
+        if j + 2 == size:
             break
-        inverse = 1.0 / pivot
-        scaled_left = row_left * inverse
-        scaled_right = row_right * inverse
+        inverse = 1.0 / det
+        solved_left = (
+            (second * left_one - cross * left_two) * inverse,
+            (first * left_two - cross * left_one) * inverse,
+        )
+        solved_right = (
+            (second * right_one - cross * right_two) * inverse,
+            lower * inverse,
+        )
         for k in range(home, tiles):
-            if k == home and r == 7:
+            if k == home and r == 6:
                 continue
-            column = jnp.broadcast_to(left[k][:, j:j + 1], (8, size))
+            columns = [jnp.broadcast_to(left[k][:, j + m:j + m + 1], (8, size)) for m in range(2)]
             if k == home:
-                column = jnp.where(sub > r, column, 0.0)
-            left[k] = left[k] - column * scaled_left
-            right[k] = right[k] - column * scaled_right
+                columns = [jnp.where(sub > r + 1, column, 0.0) for column in columns]
+            left[k] = left[k] - (columns[0] * solved_left[0] + columns[1] * solved_left[1])
+            right[k] = right[k] - (columns[0] * solved_right[0] + columns[1] * solved_right[1])
 
 
 def solve_panels(gram_ref, lead_ref, prod_ref, kernel_ref, out_ref, block, inv_one, inv_two):
@@ -76,8 +87,8 @@
 
 
 def counts_of(chunks):
-    pairs = chunks // PAIR
-    return [PAIR * (pairs // TREES + (1 if t < pairs % TREES else 0)) for t in range(TREES)]
+    groups = chunks // GROUP
+    return [GROUP * (groups // TREES + (1 if t < groups % TREES else 0)) for t in range(TREES)]
 
 
 def roles(tree, xs, y, z, planes):
@@ -125,7 +136,7 @@
     has_down = z > 0
     partner = 1 - col
 
-    head = min(HEAD, min(counts) - PAIR)
+    head = min(HEAD, min(counts) - GROUP)
     loads = []
     for t in range(TREES):
         for part, (low, size) in enumerate(((0, head), (head, counts[t] - head))):
@@ -158,7 +169,9 @@
             depth, *send = roles(t, xs, y, z, planes)
             depths[s][t] = depth
             sends[s][t] = send
-    last = planes - 1 + 4
+    deepest = [planes + 1, planes + 2, planes + 3]
+    delays = [2, 1, 0]
+    steps = max(counts[t] + SKEW * deepest[t] + delays[t] for t in range(TREES))
 
     def piece(s, t, index, size=1):
         return lead.at[s, pl.ds(starts[t] + index, size)]
@@ -197,23 +210,21 @@
                     ).start()
 
     def multiply(t, step):
-        index = step - SKEW * jnp.maximum(depths[0][t], depths[1][t])
-
-        @pl.when((index >= 0) & (index < counts[t]) & (index % PAIR == PAIR - 1))
+        index = step - SKEW * jnp.maximum(depths[0][t], depths[1][t]) - delays[t]
+
+        @pl.when((index >= 0) & (index < counts[t]) & (index % GROUP == GROUP - 1))
         def _():
-            first = starts[t] + index - (PAIR - 1)
+            first = starts[t] + index - (GROUP - 1)
             for cycle in range(cycles):
-                for b in range(PAIR):
+                for b in range(GROUP):
                     lhs[cycle * PANEL:(cycle + 1) * PANEL, b * CHUNK:(b + 1) * CHUNK] = (
                         dequantize(cycle, first + b))
             right = jnp.concatenate([
-                jnp.concatenate([lead[s, first + b] for b in range(PAIR)], axis=1)
+                jnp.concatenate([lead[s, first + b] for b in range(GROUP)], axis=1)
                 for s in range(2)], axis=0)
-            own = lhs[...]
             dims = (((1,), (1,)), ((), ()))
-            top = cycles * PANEL
-            acc[:top] += lax.dot_general(own, right, dims, preferred_element_type=jnp.float32)
-            acc[top:] += lax.dot_general(right, right, dims, preferred_element_type=jnp.float32)
+            own = jnp.concatenate([lhs[...], right], axis=0)
+            acc[...] += lax.dot_general(own, right, dims, preferred_element_type=jnp.float32)
 
     def one_step(step, carry):
         for t in range(TREES):
@@ -228,7 +239,7 @@
     lax.fori_loop(0, head, one_step, 0)
     for t in range(TREES):
         loads[2 * t + 1].wait()
-    lax.fori_loop(head, max(counts) + SKEW * last, one_step, 0)
+    lax.fori_loop(head, steps, one_step, 0)
 
     share = PANEL // 2
     top = cycles * PANEL
@@ -290,7 +301,7 @@
         scratch_shapes=[
             pltpu.VMEM((cycles, PANEL, width_local), jnp.bfloat16),
             pltpu.VMEM((2, chunks, PANEL, CHUNK), jnp.bfloat16),
-            pltpu.VMEM((cycles * PANEL, PAIR * CHUNK), jnp.bfloat16),
+            pltpu.VMEM((cycles * PANEL, GROUP * CHUNK), jnp.bfloat16),
             pltpu.VMEM((cycles * PANEL + lead_width, lead_width), jnp.float32),
             pltpu.VMEM((cycles, share_rows, lead_width), jnp.float32),
             pltpu.VMEM((lead_width, lead_width), jnp.float32),

time: 191 us -> 180 us (0.942)
  Pallas kernels: 187 us -> 176 us
    pallas_call x1, Pallas kernels: 22.9 us -> 13.4 us  [on_device(): pl.pallas_call(solve_panels, out_shape=jax.ShapeDtypeStruct((cycles * sha...]
where the time goes in v3:
time: 180 us; the launch traced here: 179 us
  Pallas kernels  176 us (98%)
  local copies, waits for them, and re-layouts  2.32 us (1%)
    pallas_call x1, Pallas kernels, on_device(): pl.pallas_call(functools.partial(gather_products, rows), out_shape=(jax.S...  163 us
    pallas_call x1, Pallas kernels, on_device(): pl.pallas_call(solve_panels, out_shape=jax.ShapeDtypeStruct((cycles * sha...  13.4 us

profile of v3, /device:TPU:29, one launch (start us, length us, event | category | flops | bytes accessed | tf_op | source)
XLA Modules:
  0.0 179.4 jit_solution(2775886675564252975)
XLA Ops:
  0.7 0.8 constant_dynamic-slice_fusion
  1.4 0.1 sub.74
  1.5 0.1 sub.78
  1.6 0.7 copy.7
  2.3 0.7 fusion.4
  3.0 0.2 select_add_fusion.1.kernel_ref
  3.2 0.2 select_add_fusion.lead_ref
  3.4 162.6 %gather_products.1 = (f32[2,64,256]{2,1,0:T(8,128)S(1)}, f32[256,256]{1,0:T(8,128)S(1)}) custom-call(bf16[2,128,32768]{2,1,0:T(8,128)(2,1)} %factor_hbm.1, f32[2,256]{1,0:T(2,128)S(1)} %bitcast.11), custom_call_target="tpu_custom_call" | custom-call | flops 17179869184 | bytes 16777216 | tf_op jit(solution)/shard_map/gather_products/pallas_call | solution.py:287
  166.0 13.4 %solve_panels.1 = f32[128,256]{1,0:T(8,128)} custom-call(f32[256,256]{1,0:T(8,128)S(1)} %get-tuple-element.7.gram_ref, f32[256,256]{1,0:T(8,128)S(1)} %select_add_fusion.lead_ref, f32[128,256]{1,0:T(8,128)S(1)} %bitcast.10, f32[128,256]{1,0:T(8,128)S(1)} %select_add_fusion.1.kernel_ref), custom_call_target="tpu_custom_call" | custom-call | tf_op jit(solution)/shard_map/solve_panels/pallas_call | solution.py:337
  (1 shorter events, 0.0 us)

commit v4 on v3

--- a/solution.py
+++ b/solution.py
@@ -9,7 +9,7 @@
 PANEL = 128
 CHUNK = 128
 GROUP = 4
-SKEW = 2
+SKEW = 3
 HEAD = 16
 
 SQRT_THREE = 1.7320508075688772

time: 180 us -> 165 us (0.917)
  Pallas kernels: 176 us -> 161 us
    pallas_call x1, Pallas kernels: 163 us -> 148 us  [on_device(): pl.pallas_call(functools.partial(gather_products, rows), out_shape=(jax.S...]
where the time goes in v4:
time: 165 us
  Pallas kernels  161 us (98%)
  local copies, waits for them, and re-layouts  2.32 us (1%)
    pallas_call x1, Pallas kernels, on_device(): pl.pallas_call(functools.partial(gather_products, rows), out_shape=(jax.S...  148 us
    pallas_call x1, Pallas kernels, on_device(): pl.pallas_call(solve_panels, out_shape=jax.ShapeDtypeStruct((cycles * sha...  13.4 us

profile of v4, /device:TPU:29, one launch (start us, length us, event | category | flops | bytes accessed | tf_op | source)
XLA Modules:
  0.0 164.7 jit_solution(441194497074706784)
XLA Ops:
  0.7 0.8 constant_dynamic-slice_fusion
  1.4 0.1 sub.74
  1.5 0.1 sub.78
  1.6 0.7 copy.7
  2.3 0.7 fusion.4
  3.0 0.2 select_add_fusion.1.kernel_ref
  3.2 0.2 select_add_fusion.lead_ref
  3.4 147.9 %gather_products.1 = (f32[2,64,256]{2,1,0:T(8,128)S(1)}, f32[256,256]{1,0:T(8,128)S(1)}) custom-call(bf16[2,128,32768]{2,1,0:T(8,128)(2,1)} %factor_hbm.1, f32[2,256]{1,0:T(2,128)S(1)} %bitcast.11), custom_call_target="tpu_custom_call" | custom-call | flops 17179869184 | bytes 16777216 | tf_op jit(solution)/shard_map/gather_products/pallas_call | solution.py:287
  151.3 13.4 %solve_panels.1 = f32[128,256]{1,0:T(8,128)} custom-call(f32[256,256]{1,0:T(8,128)S(1)} %get-tuple-element.7.gram_ref, f32[256,256]{1,0:T(8,128)S(1)} %select_add_fusion.lead_ref, f32[128,256]{1,0:T(8,128)S(1)} %bitcast.10, f32[128,256]{1,0:T(8,128)S(1)} %select_add_fusion.1.kernel_ref), custom_call_target="tpu_custom_call" | custom-call | tf_op jit(solution)/shard_map/solve_panels/pallas_call | solution.py:337
  (1 shorter events, 0.0 us)

commit v5 on v4

--- a/solution.py
+++ b/solution.py
@@ -103,14 +103,13 @@
         return z + y + xs, xs == 0, a & low, (xs == 0) & up, None
     high = jnp.logical_not(low)
     if tree == CHAIN:
-        place = jnp.where(d, 1, jnp.where(a, 2, jnp.where(b, 3, 4)))
-        depth = jnp.where(low, xs + y, z + place)
-        send_x = (low & (xs == 0)) | (high & a)
-        send_y = (low & a) | (high & (d | b))
+        depth = jnp.where(low, xs + y, z + jnp.where(d, 1, jnp.where(b, 3, 2)))
+        send_x = (low & (xs == 0)) | (high & d)
+        send_y = (low & a) | (high & (d | c))
         return depth, send_x, send_y, d & up, None
-    place = jnp.where(a, 0, jnp.where(d, 1, jnp.where(c, 2, 3)))
+    place = jnp.where(a, 0, jnp.where(c, 2, 1))
     depth = jnp.where(low, jnp.where(a, 0, place + 2), z + place)
-    return depth, high & d, high & (a | c), a & up, (z == 1) & jnp.logical_not(a)
+    return depth, high & a, high & (a | b), a & up, (z == 1) & jnp.logical_not(a)
 
 
 def gather_products(rows, factor_hbm, scales_ref, prod_ref, gram_ref,
@@ -169,8 +168,8 @@
             depth, *send = roles(t, xs, y, z, planes)
             depths[s][t] = depth
             sends[s][t] = send
-    deepest = [planes + 1, planes + 2, planes + 3]
-    delays = [2, 1, 0]
+    deepest = [planes + 1, planes + 1, planes + 2]
+    delays = [0, 1, 0]
     steps = max(counts[t] + SKEW * deepest[t] + delays[t] for t in range(TREES))
 
     def piece(s, t, index, size=1):

time: 165 us -> 162 us (0.982)
  Pallas kernels: 161 us -> 158 us
    pallas_call x1, Pallas kernels: 148 us -> 145 us  [on_device(): pl.pallas_call(functools.partial(gather_products, rows), out_shape=(jax.S...]
where the time goes in v5:
time: 162 us
  Pallas kernels  158 us (98%)
  local copies, waits for them, and re-layouts  2.32 us (1%)
    pallas_call x1, Pallas kernels, on_device(): pl.pallas_call(functools.partial(gather_products, rows), out_shape=(jax.S...  145 us
    pallas_call x1, Pallas kernels, on_device(): pl.pallas_call(solve_panels, out_shape=jax.ShapeDtypeStruct((cycles * sha...  13.4 us

profile of v5, /device:TPU:29, one launch (start us, length us, event | category | flops | bytes accessed | tf_op | source)
XLA Modules:
  0.0 161.5 jit_solution(12311287642216384452)
XLA Ops:
  0.7 0.8 constant_dynamic-slice_fusion
  1.4 0.1 sub.74
  1.5 0.1 sub.78
  1.6 0.7 copy.7
  2.3 0.7 fusion.4
  3.0 0.2 select_add_fusion.1.kernel_ref
  3.2 0.2 select_add_fusion.lead_ref
  3.4 144.7 %gather_products.1 = (f32[2,64,256]{2,1,0:T(8,128)S(1)}, f32[256,256]{1,0:T(8,128)S(1)}) custom-call(bf16[2,128,32768]{2,1,0:T(8,128)(2,1)} %factor_hbm.1, f32[2,256]{1,0:T(2,128)S(1)} %bitcast.11), custom_call_target="tpu_custom_call" | custom-call | flops 17179869184 | bytes 16777216 | tf_op jit(solution)/shard_map/gather_products/pallas_call | solution.py:286
  148.1 13.4 %solve_panels.1 = f32[128,256]{1,0:T(8,128)} custom-call(f32[256,256]{1,0:T(8,128)S(1)} %get-tuple-element.7.gram_ref, f32[256,256]{1,0:T(8,128)S(1)} %select_add_fusion.lead_ref, f32[128,256]{1,0:T(8,128)S(1)} %bitcast.10, f32[128,256]{1,0:T(8,128)S(1)} %select_add_fusion.1.kernel_ref), custom_call_target="tpu_custom_call" | custom-call | tf_op jit(solution)/shard_map/solve_panels/pallas_call | solution.py:336
  (1 shorter events, 0.0 us)

commit v6 on v5

--- a/solution.py
+++ b/solution.py
@@ -10,7 +10,7 @@
 CHUNK = 128
 GROUP = 4
 SKEW = 3
-HEAD = 16
+HEAD = 8
 
 SQRT_THREE = 1.7320508075688772
 LENGTH_SCALE = 0.25
@@ -195,7 +195,7 @@
             def _():
                 pltpu.make_async_copy(here, here, recv_sem.at[s, t, index]).wait()
 
-            for way in range(4):
+            for way in (2, 3, 0, 1):
                 wanted = sends[s][t][way]
                 if wanted is None:
                     continue
@@ -226,7 +226,7 @@
             acc[...] += lax.dot_general(own, right, dims, preferred_element_type=jnp.float32)
 
     def one_step(step, carry):
-        for t in range(TREES):
+        for t in (CHAIN, LIFT, TWIN):
             for s in range(2):
                 forward(s, t, step)
         for t in range(TREES):

time: 162 us -> 161 us (level)
  no operation moved by 1% of the time
where the time goes in v6:
time: 161 us
  Pallas kernels  157 us (98%)
  local copies, waits for them, and re-layouts  2.32 us (1%)
    pallas_call x1, Pallas kernels, on_device(): pl.pallas_call(functools.partial(gather_products, rows), out_shape=(jax.S...  144 us
    pallas_call x1, Pallas kernels, on_device(): pl.pallas_call(solve_panels, out_shape=jax.ShapeDtypeStruct((cycles * sha...  13.4 us

profile of v6, /device:TPU:29, one launch (start us, length us, event | category | flops | bytes accessed | tf_op | source)
XLA Modules:
  0.0 160.6 jit_solution(5275837522580972083)
XLA Ops:
  0.7 0.8 constant_dynamic-slice_fusion
  1.4 0.1 sub.74
  1.5 0.1 sub.78
  1.6 0.7 copy.7
  2.3 0.7 fusion.4
  3.0 0.2 select_add_fusion.1.kernel_ref
  3.2 0.2 select_add_fusion.lead_ref
  3.4 143.8 %gather_products.1 = (f32[2,64,256]{2,1,0:T(8,128)S(1)}, f32[256,256]{1,0:T(8,128)S(1)}) custom-call(bf16[2,128,32768]{2,1,0:T(8,128)(2,1)} %factor_hbm.1, f32[2,256]{1,0:T(2,128)S(1)} %bitcast.11), custom_call_target="tpu_custom_call" | custom-call | flops 17179869184 | bytes 16777216 | tf_op jit(solution)/shard_map/gather_products/pallas_call | solution.py:286
  147.2 13.4 %solve_panels.1 = f32[128,256]{1,0:T(8,128)} custom-call(f32[256,256]{1,0:T(8,128)S(1)} %get-tuple-element.7.gram_ref, f32[256,256]{1,0:T(8,128)S(1)} %select_add_fusion.lead_ref, f32[128,256]{1,0:T(8,128)S(1)} %bitcast.10, f32[128,256]{1,0:T(8,128)S(1)} %select_add_fusion.1.kernel_ref), custom_call_target="tpu_custom_call" | custom-call | tf_op jit(solution)/shard_map/solve_panels/pallas_call | solution.py:336
  (1 shorter events, 0.0 us)
